TPU v7x, 32 devices: a whole 2x2x4 slice. The times are simulated.
32 devices in a mesh: dp: 4 (over x, core), group: 8 (over z, y).
Axes of the slice: x: 2, y: 2, z: 4, core: 2. Of those that a mesh axis runs over, the one named last changes fastest.
Arguments:
- embeds: bfloat16 [8192, 1024], P(('dp', 'group')), may hold values from -6 to 6
- row_ids: int32 [8192], P(('dp', 'group')), may hold values from 0 to 63
- neighbors: int32 [32, 3], P('dp'), may hold values from 0 to 7, as said below
- w_first: bfloat16 [1024, 4096], P(None, 'dp'), may hold values from -0.1875 to 0.1875
- w_second: bfloat16 [4096, 1024], P('dp'), may hold values from -0.09375 to 0.09375
Outputs:
- grad_first: float32 [1024, 4096], P('group', 'dp')
- grad_second: float32 [4096, 1024], P('dp', 'group')
- grad_unit: float32 [8192, 1024], P(('dp', 'group'))
Inputs may be any that keep to these rules, and one draw needn't show every extreme that they name: `neighbors`: within a row the 3 entries differ from one another and from the row's own index b % 8.
All inputs are finite; a program needn't handle non-finite values.
Results may differ from a plain program's by a relative error of at most 0.013.
Values may be sent and summed in bfloat16 or wider, within the bound.
A program may use at most 64 MiB of HBM per device.

v0:
```python
import jax
import jax.numpy as jnp
from jax import lax
from jax.sharding import PartitionSpec as P

EPS = 1e-06
TEMP = 10.0
SHIFT = -5.0


def gelu_fwd(value):
    return jax.nn.gelu(value, approximate=True)


def gelu_back(pre, grad):
    _, back = jax.vjp(gelu_fwd, pre)
    return back(grad)[0]


def per_device(embeds, row_ids, neighbors, w_first, w_second):
    owners = lax.axis_size("group")
    block = embeds.shape[0]
    piece = block // owners
    width = w_second.shape[1]
    listed = neighbors.shape[1]
    gathered = lax.all_gather(embeds, "dp", axis=0, tiled=True)
    pre = jnp.dot(gathered, w_first, preferred_element_type=jnp.float32)
    hidden = gelu_fwd(pre).astype(jnp.bfloat16)
    proj = lax.psum_scatter(
        jnp.dot(hidden, w_second, preferred_element_type=jnp.float32).astype(jnp.bfloat16),
        "dp",
        scatter_dimension=0,
        tiled=True,
    ).astype(jnp.float32)
    inv = lax.rsqrt(jnp.mean(proj * proj, axis=-1, keepdims=True) + EPS)
    unit = proj * inv
    unit_b = unit.astype(jnp.bfloat16)
    held, held_ids = (
        lax.all_to_all(
            unit_b.reshape(owners, piece, width), "group", split_axis=0, concat_axis=0, tiled=True
        ),
        lax.all_to_all(
            row_ids.reshape(owners, piece), "group", split_axis=0, concat_axis=0, tiled=True
        ),
    )
    order = neighbors.T
    outgoing = jnp.take(held, order, axis=0)
    outgoing_ids = jnp.take(held_ids, order, axis=0)
    fetched, fetched_ids = (
        lax.all_to_all(outgoing, "group", split_axis=1, concat_axis=1, tiled=True),
        lax.all_to_all(outgoing_ids, "group", split_axis=1, concat_axis=1, tiled=True),
    )
    cand = jnp.concatenate([unit_b[None], fetched.reshape(listed, block, width)], 0)
    cand_ids = jnp.concatenate([row_ids[None], fetched_ids.reshape(listed, block)], 0)
    logits = (
        TEMP / width * jnp.einsum("rp,kcp->krc", unit_b, cand, preferred_element_type=jnp.float32)
        + SHIFT
    )
    sign = jnp.where(row_ids[None, :, None] == cand_ids[:, None, :], 1.0, -1.0).astype(jnp.float32)
    weight = (-sign * jax.nn.sigmoid(-sign * logits) * (TEMP / width)).astype(jnp.bfloat16)
    grad_own = jnp.einsum("krc,kcp->rp", weight, cand, preferred_element_type=jnp.float32)
    grad_cand = jnp.einsum("krc,rp->kcp", weight, unit_b, preferred_element_type=jnp.float32)
    returned = lax.all_to_all(
        grad_cand[1:].reshape(listed, owners, piece, width),
        "group",
        split_axis=1,
        concat_axis=1,
        tiled=True,
    )
    select = (order[:, :, None] == jnp.arange(owners, dtype=jnp.int32)[None, None, :]).astype(
        jnp.float32
    )
    summed = jnp.einsum("krb,krqp->bqp", select, returned, precision=lax.Precision.HIGHEST)
    collected = lax.all_to_all(summed, "group", split_axis=0, concat_axis=0, tiled=True)
    grad_unit = grad_own + grad_cand[0] + collected.reshape(block, width)
    grad_proj = inv * (grad_unit - unit * jnp.mean(unit * grad_unit, axis=-1, keepdims=True))
    grad_all = lax.all_gather(grad_proj.astype(jnp.bfloat16), "dp", axis=0, tiled=True)
    second_local = lax.dot_general(
        hidden, grad_all, (((0,), (0,)), ((), ())), preferred_element_type=jnp.float32
    )
    grad_hidden = lax.dot_general(
        grad_all, w_second, (((1,), (1,)), ((), ())), preferred_element_type=jnp.float32
    )
    grad_pre = gelu_back(pre, grad_hidden).astype(jnp.bfloat16)
    first_local = lax.dot_general(
        gathered, grad_pre, (((0,), (0,)), ((), ())), preferred_element_type=jnp.float32
    )
    first_out, second_out = (
        lax.psum_scatter(first_local, "group", scatter_dimension=0, tiled=True),
        lax.psum_scatter(second_local, "group", scatter_dimension=1, tiled=True),
    )
    return (first_out, second_out, grad_unit)


def solution(mesh):
    in_specs = (
        P(("dp", "group"), None),
        P(("dp", "group")),
        P("dp", None),
        P(None, "dp"),
        P("dp", None),
    )
    out_specs = (P("group", "dp"), P("dp", "group"), P(("dp", "group"), None))
    return jax.shard_map(
        per_device, mesh=mesh, in_specs=in_specs, out_specs=out_specs, check_vma=False
    )
```

profile of v0, /device:TPU:0, one launch (start us, length us, event | category | flops | bytes accessed | tf_op | source)
XLA Modules:
  0.0 487.5 jit_solution(14906962137493817778)
XLA Ops:
  8.0 26.9 %all-gather.3.cloned.1.call-done = bf16[1024,1024]{1,0:T(8,128)(2,1)} async-done(((bf16[256,1024]{1,0:T(8,128)(2,1)}), bf16[1024,1024]{1,0:T(8,128)(2,1)}) %all-gather.3.cloned.1.call-update) | async-done | bytes 2097168 | tf_op jit(solution)/shard_map/all_gather | solution.py:26
  34.9 4.5 fusion.50
  39.5 1.9 copy-done.5
  41.4 4.0 convolution_convert_fusion
  46.1 5.5 %all-to-all-start = ((s32[8,1,32]{2,1,0:T(1,128)}), s32[8,1,32]{2,1,0:T(1,128)S(1)}, u32[]{:S(2)}, u32[]{:S(2)}) async-start(s32[8,1,32]{2,1,0:T(1,128)} %all_to_all.23), calls=%async_computation.1 | async-start | bytes 8192 | tf_op jit(solution)/shard_map/all_to_all | solution.py:42
  51.7 25.4 %reduce-scatter.4.cloned.1.call-done = bf16[256,1024]{1,0:T(8,128)(2,1)} async-done(((bf16[1024,1024]{1,0:T(8,128)(2,1)}), bf16[256,1024]{1,0:T(8,128)(2,1)}) %reduce-scatter.4.cloned.1.call-update) | async-done | bytes 524304 | tf_op jit(solution)/shard_map/reduce_scatter | solution.py:29
  78.3 2.0 fusion.23
  80.3 5.5 %all-to-all-start.2 = ((bf16[8,32,1024]{2,1,0:T(8,128)(2,1)}), bf16[8,32,1024]{2,1,0:T(8,128)(2,1)S(1)}, u32[]{:S(2)}, u32[]{:S(2)}) async-start(bf16[8,32,1024]{2,1,0:T(8,128)(2,1)} %bitcast.5), calls=%async_computation.3 | async-start | bytes 1048576 | tf_op jit(solution)/shard_map/all_to_all | solution.py:39
  87.2 13.0 %all-to-all-done.2 = bf16[8,32,1024]{2,1,0:T(8,128)(2,1)S(1)} async-done(((bf16[8,32,1024]{2,1,0:T(8,128)(2,1)}), bf16[8,32,1024]{2,1,0:T(8,128)(2,1)S(1)}, u32[]{:S(2)}, u32[]{:S(2)}) %all-to-all-start.2) | async-done | bytes 524320 | tf_op jit(solution)/shard_map/all_to_all | solution.py:39
  100.3 3.6 all-to-all-start.1
  103.9 1.9 gather_fusion.1
  110.5 4.3 all-to-all-start.3
  115.1 36.4 %all-to-all-done.3 = bf16[3,8,32,1024]{3,2,0,1:T(8,128)(2,1)} async-done(((bf16[3,8,32,1024]{3,2,0,1:T(8,128)(2,1)}), bf16[3,8,32,1024]{3,2,0,1:T(8,128)(2,1)}, u32[]{:S(2)}, u32[]{:S(2)}) %all-to-all-start.3) | async-done | bytes 1572896 | tf_op jit(solution)/shard_map/all_to_all | solution.py:50
  153.0 2.3 fusion.27
  155.3 1.8 fusion.33
  157.9 74.3 %all_to_all.37 = f32[3,8,32,1024]{3,2,0,1:T(8,128)S(1)} all-to-all(f32[3,8,32,1024]{3,2,0,1:T(8,128)S(1)} %copy.41), channel_id=1, replica_groups=mesh['dp'=4,'group'=8] {'group'}, dimensions={1} | all-to-all | bytes 6291456 | tf_op jit(solution)/shard_map/all_to_all | solution.py:63
  232.1 2.9 fusion.10
  235.7 28.9 %all_to_all.38 = f32[8,32,1024]{2,1,0:T(8,128)S(1)} all-to-all(f32[8,32,1024]{2,1,0:T(8,128)S(1)} %copy.43), channel_id=1, replica_groups=mesh['dp'=4,'group'=8] {'group'}, dimensions={0} | all-to-all | bytes 2097152 | tf_op jit(solution)/shard_map/all_to_all | solution.py:74
  267.6 20.7 %all-gather.5.cloned.1.call-done = bf16[1024,1024]{1,0:T(8,128)(2,1)} async-done(((bf16[256,1024]{1,0:T(8,128)(2,1)}), bf16[1024,1024]{1,0:T(8,128)(2,1)}) %all-gather.5.cloned.1.call-update) | async-done | bytes 2097168 | tf_op jit(solution)/shard_map/all_gather | solution.py:77
  288.3 11.7 %convolution_bitcast_fusion = f32[1024,1024]{0,1:T(8,128)} fusion(bf16[1024,1024]{1,0:T(8,128)(2,1)} %all-gather.3.cloned.1.call-done, f32[1024,1024]{1,0:T(8,128)} %copy-done.5, bf16[1024,1024]{1,0:T(8,128)(2,1)} %all-gather.5.cloned.1.call-done, bf16[1024,1024]{1,0:T(8,128)(2,1)S(1)} %copy-done), kind=kOutput, calls=%fused_computation.14 | convolution fusion | flops 4315938816 | bytes 14680064 | tf_op jit(solution)/shard_map/dot_general | solution.py:85
  300.1 7.6 %fusion.47 = f32[1024,1024]{1,0:T(8,128)} fusion(bf16[1024,1024]{1,0:T(8,128)(2,1)} %all-gather.5.cloned.1.call-done, f32[1024,1024]{1,0:T(8,128)} %copy-done.5), kind=kOutput, calls=%fused_computation.65 | convolution fusion | flops 2156920832 | bytes 10485760 | tf_op jit(solution)/shard_map/dot_general | solution.py:78
  307.7 80.9 %reduce-scatter.6.cloned.1.call-done = f32[128,1024]{0,1:T(8,128)} async-done(((f32[1024,1024]{0,1:T(8,128)}), f32[128,1024]{0,1:T(8,128)}) %reduce-scatter.6.cloned.1.call-update) | async-done | bytes 524304 | tf_op jit(solution)/shard_map/reduce_scatter | solution.py:89
  388.6 2.0 copy.44
  390.7 90.3 %reduce-scatter.8.cloned.1.call-done = f32[1024,128]{1,0:T(8,128)} async-done(((f32[1024,1024]{1,0:T(8,128)}), f32[1024,128]{1,0:T(8,128)}) %reduce-scatter.8.cloned.1.call-update) | async-done | bytes 524304 | tf_op jit(solution)/shard_map/reduce_scatter | solution.py:90
  (46 shorter events, 15.2 us)
Async XLA Ops:
  7.2 34.2 %copy-start = (bf16[1024,1024]{1,0:T(8,128)(2,1)S(1)}, bf16[1024,1024]{1,0:T(8,128)(2,1)}, u32[]{:S(2)}) copy-start(bf16[1024,1024]{1,0:T(8,128)(2,1)} %param.9) | copy-start | bytes 6291460
  7.2 27.7 %all-gather.3.cloned.1.call-start = ((), (), s32[]{:S(2)}) async-start(), calls=%async_computation.9 | async-start | bytes 2621440 | tf_op jit(solution)/shard_map/all_gather | solution.py:26
  7.9 69.1 %reduce-scatter.4.cloned.1.call-start = ((), (), s32[]{:S(2)}) async-start(), calls=%async_computation.10 | async-start | bytes 2621440 | tf_op jit(solution)/shard_map/reduce_scatter | solution.py:29
  39.4 2.0 copy-start.5
  41.4 4.0 copy-start.4
  45.4 40.4 %copy-start.3 = (s32[8,3]{0,1:T(4,128)S(1)}, s32[8,3]{0,1:T(4,128)}, u32[]{:S(2)}) copy-start(s32[8,3]{0,1:T(4,128)} %param.7) | copy-start | bytes 292
  46.1 34.1 %all-to-all-start = ((s32[8,1,32]{2,1,0:T(1,128)}), s32[8,1,32]{2,1,0:T(1,128)S(1)}, u32[]{:S(2)}, u32[]{:S(2)}) async-start(s32[8,1,32]{2,1,0:T(1,128)} %all_to_all.23), calls=%async_computation.1 | async-start | bytes 8192 | tf_op jit(solution)/shard_map/all_to_all | solution.py:42
  80.3 20.0 %all-to-all-start.2 = ((bf16[8,32,1024]{2,1,0:T(8,128)(2,1)}), bf16[8,32,1024]{2,1,0:T(8,128)(2,1)S(1)}, u32[]{:S(2)}, u32[]{:S(2)}) async-start(bf16[8,32,1024]{2,1,0:T(8,128)(2,1)} %bitcast.5), calls=%async_computation.3 | async-start | bytes 1048576 | tf_op jit(solution)/shard_map/all_to_all | solution.py:39
  100.3 10.2 %all-to-all-start.1 = ((s32[3,8,32]{2,0,1:T(4,128)}), s32[3,8,32]{2,0,1:T(4,128)S(1)}, u32[]{:S(2)}, u32[]{:S(2)}) async-start(s32[3,8,32]{2,0,1:T(4,128)} %copy_select_fusion), calls=%async_computation.2 | async-start | bytes 32768 | tf_op jit(solution)/shard_map/all_to_all | solution.py:51
  105.8 9.1 %copy-start.1 = (bf16[256,1024]{1,0:T(8,128)(2,1)S(1)}, bf16[256,1024]{1,0:T(8,128)(2,1)}, u32[]{:S(2)}) copy-start(bf16[256,1024]{1,0:T(8,128)(2,1)} %reduce-scatter.4.cloned.1.call-done) | copy-start | bytes 1572868
  110.5 41.0 %all-to-all-start.3 = ((bf16[3,8,32,1024]{3,2,0,1:T(8,128)(2,1)}), bf16[3,8,32,1024]{3,2,0,1:T(8,128)(2,1)}, u32[]{:S(2)}, u32[]{:S(2)}) async-start(bf16[3,8,32,1024]{3,2,0,1:T(8,128)(2,1)} %copy.37), calls=%async_computation.4 | async-start | bytes 3145728 | tf_op jit(solution)/shard_map/all_to_all | solution.py:50
  114.8 173.5 %all-gather.5.cloned.1.call-start = ((), (), s32[]{:S(2)}) async-start(), calls=%async_computation.11 | async-start | bytes 2621440 | tf_op jit(solution)/shard_map/all_gather | solution.py:77
  265.5 1.0 copy-start.2
  267.5 121.1 %reduce-scatter.6.cloned.1.call-start = ((), (), s32[]{:S(2)}) async-start(), calls=%async_computation.12 | async-start | bytes 4718592 | tf_op jit(solution)/shard_map/reduce_scatter | solution.py:89
  300.0 180.9 %reduce-scatter.8.cloned.1.call-start = ((), (), s32[]{:S(2)}) async-start(), calls=%async_computation.13 | async-start | bytes 4718592 | tf_op jit(solution)/shard_map/reduce_scatter | solution.py:90
Sparse Core Ops, SparseCore 0:
  9.6 25.2 all-gather.2
  45.6 31.4 reduce-scatter.3
  267.7 20.6 all-gather.4
  300.2 88.4 reduce-scatter.5
  392.7 88.1 reduce-scatter.7
where the time goes:
time: 488 us; the launch traced here: 487 us
  waiting for transfers between devices  296 us (61%)
  blocking collectives  103 us (21%)
  matrix products  35.7 us (7%)
  starting transfers between devices  19.2 us (4%)
  between operations  13.9 us (3%)
  local copies, waits for them, and re-layouts  12.6 us (3%)
  other arithmetic  6.81 us (1%)
    reduce_scatter x1, waiting for transfers between devices, per_device(): lax.psum_scatter(second_local, 'group', scatter_dimension=1, tiled=True)  90.3 us
    reduce_scatter x1, waiting for transfers between devices, per_device(): lax.psum_scatter(first_local, 'group', scatter_dimension=0, tiled=True)  80.9 us
    all_to_all x1, blocking collectives, per_device(): lax.all_to_all(grad_cand[1:].reshape(listed, owners, piece, width), 'grou...  74.3 us
    all_to_all x1, waiting for transfers between devices, per_device(): lax.all_to_all(outgoing, 'group', split_axis=1, concat_axis=1, tiled=True)  36.4 us
    all_to_all x1, blocking collectives, per_device(): lax.all_to_all(summed, 'group', split_axis=0, concat_axis=0, tiled=True)  28.9 us
    all_gather x1, waiting for transfers between devices, per_device(): gathered = lax.all_gather(embeds, 'dp', axis=0, tiled=True)  26.9 us
    reduce_scatter x1, waiting for transfers between devices, per_device(): lax.psum_scatter(jnp.dot(hidden, w_second, preferred_element_type=jnp.flo...  25.4 us
    all_gather x1, waiting for transfers between devices, per_device(): lax.all_gather(grad_proj.astype(jnp.bfloat16), 'dp', axis=0, tiled=True)  20.7 us
  transfers between devices with their start and end apart: 9, of which 8 were waited for; matrix products, arithmetic and copies ran while one was open for 4% of the time, Pallas kernels for 0%

commit v1 on v0

v1 whole, which is shorter than its diff:
```python
import jax
import jax.numpy as jnp
from jax import lax
from jax.sharding import PartitionSpec as P

EPS = 1e-06
TEMP = 10.0
SHIFT = -5.0


def gelu_fwd(value):
    return jax.nn.gelu(value, approximate=True)


def gelu_back(pre, grad):
    _, back = jax.vjp(gelu_fwd, pre)
    return back(grad)[0]


def per_device(embeds, row_ids, neighbors, w_first, w_second):
    owners = lax.axis_size("group")
    block = embeds.shape[0]
    width = w_second.shape[1]
    gathered = lax.all_gather(embeds, "dp", axis=0, tiled=True)
    pre = jnp.dot(gathered, w_first, preferred_element_type=jnp.float32)
    hidden = gelu_fwd(pre).astype(jnp.bfloat16)
    proj = lax.psum_scatter(
        jnp.dot(hidden, w_second, preferred_element_type=jnp.float32).astype(jnp.bfloat16),
        "dp",
        scatter_dimension=0,
        tiled=True,
    ).astype(jnp.float32)
    inv = lax.rsqrt(jnp.mean(proj * proj, axis=-1, keepdims=True) + EPS)
    unit = proj * inv
    unit_b = unit.astype(jnp.bfloat16)
    units = lax.all_gather(unit_b, "group", axis=0, tiled=True)
    ids = lax.all_gather(row_ids, "group", axis=0, tiled=True)
    me = lax.axis_index("group")
    others = jnp.arange(owners, dtype=jnp.int32)
    mine = lax.dynamic_index_in_dim(neighbors, me, 0, keepdims=False)
    lists = jnp.sum((mine[None, :] == others[:, None]).astype(jnp.float32), axis=1)
    listed_by = jnp.sum((neighbors == me).astype(jnp.float32), axis=1)
    times = jnp.where(others == me, 2.0, lists + listed_by)
    times = jnp.repeat(times, block)[None, :]
    logits = (
        TEMP
        / width
        * lax.dot_general(
            unit_b, units, (((1,), (1,)), ((), ())), preferred_element_type=jnp.float32
        )
        + SHIFT
    )
    sign = jnp.where(row_ids[:, None] == ids[None, :], 1.0, -1.0).astype(jnp.float32)
    weight = (-sign * jax.nn.sigmoid(-sign * logits) * (TEMP / width)).astype(jnp.bfloat16)
    weight = weight * times.astype(jnp.bfloat16)
    grad_unit = jnp.dot(weight, units, preferred_element_type=jnp.float32)
    grad_proj = inv * (grad_unit - unit * jnp.mean(unit * grad_unit, axis=-1, keepdims=True))
    grad_all = lax.all_gather(grad_proj.astype(jnp.bfloat16), "dp", axis=0, tiled=True)
    second_local = lax.dot_general(
        hidden, grad_all, (((0,), (0,)), ((), ())), preferred_element_type=jnp.float32
    )
    grad_hidden = lax.dot_general(
        grad_all, w_second, (((1,), (1,)), ((), ())), preferred_element_type=jnp.float32
    )
    grad_pre = gelu_back(pre, grad_hidden).astype(jnp.bfloat16)
    first_local = lax.dot_general(
        gathered, grad_pre, (((0,), (0,)), ((), ())), preferred_element_type=jnp.float32
    )
    first_out, second_out = (
        lax.psum_scatter(first_local, "group", scatter_dimension=0, tiled=True),
        lax.psum_scatter(second_local, "group", scatter_dimension=1, tiled=True),
    )
    return (first_out, second_out, grad_unit)


def solution(mesh):
    in_specs = (
        P(("dp", "group"), None),
        P(("dp", "group")),
        P("dp", None),
        P(None, "dp"),
        P("dp", None),
    )
    out_specs = (P("group", "dp"), P("dp", "group"), P(("dp", "group"), None))
    return jax.shard_map(
        per_device, mesh=mesh, in_specs=in_specs, out_specs=out_specs, check_vma=False
    )
```

time: 488 us -> 384 us (0.79)
  blocking collectives: 103 us -> 20.6 us
  starting transfers between devices: 19.2 us -> 0.42 us
  local copies, waits for them, and re-layouts: 12.6 us -> 4.25 us
  waiting for transfers between devices: 296 us -> 304 us
    all_to_all x2 -> x0, blocking collectives: 103 us -> none  [the longest x1 74.3 us: per_device(): lax.all_to_all(grad_cand[1:].reshape(listed, owners, piece, width), 'grou...]
    all_gather x0 -> x1, waiting for transfers between devices: none -> 52.5 us  [per_device(): units = lax.all_gather(unit_b, 'group', axis=0, tiled=True)]
    all_to_all x4 -> x0, waiting for transfers between devices: 51.1 us -> none  [the longest x1 36.4 us: per_device(): lax.all_to_all(outgoing, 'group', split_axis=1, concat_axis=1, tiled=True)]
    all_gather x0 -> x1, blocking collectives: none -> 20.6 us  [per_device(): ids = lax.all_gather(row_ids, 'group', axis=0, tiled=True)]
    all_to_all x4 -> x0, starting transfers between devices: 19 us -> none  [the longest x1 5.52 us: per_device(): lax.all_to_all(unit_b.reshape(owners, piece, width), 'group', split_axis=...]
    reduce_scatter x1, waiting for transfers between devices: 25.4 us -> 31.5 us  [per_device(): lax.psum_scatter(jnp.dot(hidden, w_second, preferred_element_type=jnp.flo...]
  transfers between devices with their start and end apart: 9 -> 6, of which waited for: 8 -> 6; matrix products, arithmetic and copies ran while one was open for 4% -> 3% of each run, Pallas kernels for 0% -> 0%
where the time goes in v1:
time: 384 us
  waiting for transfers between devices  304 us (79%)
  matrix products  35.2 us (9%)
  blocking collectives  20.6 us (5%)
  between operations  14.2 us (4%)
  other arithmetic  5.6 us (1%)
  local copies, waits for them, and re-layouts  4.25 us (1%)
    reduce_scatter x1, waiting for transfers between devices, per_device(): lax.psum_scatter(second_local, 'group', scatter_dimension=1, tiled=True)  90.3 us
    reduce_scatter x1, waiting for transfers between devices, per_device(): lax.psum_scatter(first_local, 'group', scatter_dimension=0, tiled=True)  80.8 us
    all_gather x1, waiting for transfers between devices, per_device(): units = lax.all_gather(unit_b, 'group', axis=0, tiled=True)  52.5 us
    reduce_scatter x1, waiting for transfers between devices, per_device(): lax.psum_scatter(jnp.dot(hidden, w_second, preferred_element_type=jnp.flo...  31.5 us
    all_gather x1, waiting for transfers between devices, per_device(): gathered = lax.all_gather(embeds, 'dp', axis=0, tiled=True)  26.9 us
    all_gather x1, waiting for transfers between devices, per_device(): lax.all_gather(grad_proj.astype(jnp.bfloat16), 'dp', axis=0, tiled=True)  20.8 us
    all_gather x1, blocking collectives, per_device(): ids = lax.all_gather(row_ids, 'group', axis=0, tiled=True)  20.6 us
    dot_general x1, matrix products, per_device(): lax.dot_general(gathered, grad_pre, (((0,), (0,)), ((), ())), preferred_e...  11.7 us
  transfers between devices with their start and end apart: 6, of which 6 were waited for; matrix products, arithmetic and copies ran while one was open for 3% of the time, Pallas kernels for 0%

profile of v1, /device:TPU:0, one launch (start us, length us, event | category | flops | bytes accessed | tf_op | source)
XLA Modules:
  0.0 383.9 jit_solution(17410591213497206218)
XLA Ops:
  7.2 0.7 all-gather.5.cloned.1.call-update
  8.0 26.9 %all-gather.5.cloned.1.call-done = bf16[1024,1024]{1,0:T(8,128)(2,1)} async-done(((bf16[256,1024]{1,0:T(8,128)(2,1)}), bf16[1024,1024]{1,0:T(8,128)(2,1)}) %all-gather.5.cloned.1.call-update) | async-done | bytes 2097168 | tf_op jit(solution)/shard_map/all_gather | solution.py:24
  34.9 4.5 %fusion.50 = f32[1024,1024]{1,0:T(8,128)S(1)} fusion(bf16[1024,1024]{1,0:T(8,128)(2,1)} %all-gather.5.cloned.1.call-done, bf16[1024,1024]{1,0:T(8,128)(2,1)} %param.8), kind=kOutput, calls=%fused_computation.62 | convolution fusion | flops 2147483648 | bytes 8388608 | tf_op jit(solution)/shard_map/dot_general | solution.py:25
  39.5 1.9 copy-done.4
  41.4 4.0 %convolution_convert_fusion = bf16[1024,1024]{1,0:T(8,128)(2,1)} fusion(bf16[1024,1024]{1,0:T(8,128)(2,1)S(1)} %copy-done, f32[1024,1024]{1,0:T(8,128)S(1)} %fusion.50), kind=kOutput, calls=%fused_computation.22 | convolution fusion | flops 2157969408 | bytes 8388608 | tf_op jit(solution)/shard_map/dot_general | solution.py:28
  45.4 0.0 all-gather.7.cloned.1.call-start
  45.5 31.5 %reduce-scatter.4.cloned.1.call-done = bf16[256,1024]{1,0:T(8,128)(2,1)} async-done(((bf16[1024,1024]{1,0:T(8,128)(2,1)}), bf16[256,1024]{1,0:T(8,128)(2,1)}) %reduce-scatter.4.cloned.1.call-update) | async-done | bytes 524304 | tf_op jit(solution)/shard_map/reduce_scatter | solution.py:27
  77.0 1.2 fusion.26
  78.2 2.0 fusion.20
  80.2 0.0 all-gather.9.cloned.1.call-start
  80.3 0.2 dynamic-slice_reduce_fusion
  80.5 0.1 convert_reduce_fusion
  80.6 0.1 broadcast_bitcast_fusion
  80.7 20.6 %all-gather = s32[8,1,256]{2,1,0:T(1,128)S(1)} all-gather(s32[1,1,256]{2,1,0:T(1,128)S(1)} %bitcast.18), channel_id=1, replica_groups=mesh['dp'=4,'group'=8] {'group'}, dimensions={0}, use_global_device_ids=true | all-gather | bytes 9216 | tf_op jit(solution)/shard_map/all_gather | solution.py:37
  101.3 52.5 %all-gather.7.cloned.1.call-done = bf16[2048,1024]{1,0:T(8,128)(2,1)} async-done(((bf16[256,1024]{1,0:T(8,128)(2,1)}), bf16[2048,1024]{1,0:T(8,128)(2,1)}) %all-gather.7.cloned.1.call-update) | async-done | bytes 4194320 | tf_op jit(solution)/shard_map/all_gather | solution.py:36
  153.8 7.4 %fusion.22 = (f32[256]{0:T(256)S(1)}, f32[256,1024]{1,0:T(8,128)}) fusion(bf16[256,1024]{1,0:T(8,128)(2,1)} %reduce-scatter.4.cloned.1.call-done, f32[256]{0:T(256)S(1)} %add_rsqrt_fusion, bf16[2048,1024]{1,0:T(8,128)(2,1)} %all-gather.7.cloned.1.call-done, s32[2048]{0:T(1024)S(1)} %bitcast.16, s32[256]{0:T(256)S(1)} %copy-done.3, ...), kind=kOutput, calls=%fused_computation.29 | convolution fusion | flops 2156134144 | bytes 5782528 | tf_op jit(solution)/shard_map/dot_general | solution.py:56
  161.2 2.3 fusion.25
  163.5 0.2 reduce-scatter.6.cloned.1.call-start
  163.8 20.8 %all-gather.9.cloned.1.call-done = bf16[1024,1024]{1,0:T(8,128)(2,1)} async-done(((bf16[256,1024]{1,0:T(8,128)(2,1)}), bf16[1024,1024]{1,0:T(8,128)(2,1)}) %all-gather.9.cloned.1.call-update) | async-done | bytes 2097168 | tf_op jit(solution)/shard_map/all_gather | solution.py:58
  184.5 11.7 %convolution_bitcast_fusion = f32[1024,1024]{0,1:T(8,128)} fusion(bf16[1024,1024]{1,0:T(8,128)(2,1)} %all-gather.5.cloned.1.call-done, f32[1024,1024]{1,0:T(8,128)} %copy-done.4, bf16[1024,1024]{1,0:T(8,128)(2,1)} %all-gather.9.cloned.1.call-done, bf16[1024,1024]{1,0:T(8,128)(2,1)S(1)} %copy-done), kind=kOutput, calls=%fused_computation.21 | convolution fusion | flops 4315938816 | bytes 14680064 | tf_op jit(solution)/shard_map/dot_general | solution.py:66
  196.3 7.6 %fusion.45 = f32[1024,1024]{1,0:T(8,128)} fusion(bf16[1024,1024]{1,0:T(8,128)(2,1)} %all-gather.9.cloned.1.call-done, f32[1024,1024]{1,0:T(8,128)} %copy-done.4), kind=kOutput, calls=%fused_computation.60 | convolution fusion | flops 2156920832 | bytes 10485760 | tf_op jit(solution)/shard_map/dot_general | solution.py:59
  203.9 80.8 %reduce-scatter.6.cloned.1.call-done = f32[128,1024]{0,1:T(8,128)} async-done(((f32[1024,1024]{0,1:T(8,128)}), f32[128,1024]{0,1:T(8,128)}) %reduce-scatter.6.cloned.1.call-update) | async-done | bytes 524304 | tf_op jit(solution)/shard_map/reduce_scatter | solution.py:70
  284.7 2.0 copy.10
  286.7 90.3 %reduce-scatter.8.cloned.1.call-done = f32[1024,128]{1,0:T(8,128)} async-done(((f32[1024,1024]{1,0:T(8,128)}), f32[1024,128]{1,0:T(8,128)}) %reduce-scatter.8.cloned.1.call-update) | async-done | bytes 524304 | tf_op jit(solution)/shard_map/reduce_scatter | solution.py:71
  (21 shorter events, 0.3 us)
Async XLA Ops:
  7.2 34.2 %copy-start = (bf16[1024,1024]{1,0:T(8,128)(2,1)S(1)}, bf16[1024,1024]{1,0:T(8,128)(2,1)}, u32[]{:S(2)}) copy-start(bf16[1024,1024]{1,0:T(8,128)(2,1)} %param.9) | copy-start | bytes 6291460
  7.2 27.7 %all-gather.5.cloned.1.call-start = ((), (), s32[]{:S(2)}) async-start(), calls=%async_computation.3 | async-start | bytes 2621440 | tf_op jit(solution)/shard_map/all_gather | solution.py:24
  7.9 69.1 %reduce-scatter.4.cloned.1.call-start = ((), (), s32[]{:S(2)}) async-start(), calls=%async_computation.4 | async-start | bytes 2621440 | tf_op jit(solution)/shard_map/reduce_scatter | solution.py:27
  39.4 1.9 copy-start.4
  45.4 34.9 %copy-start.2 = (s32[8,3]{0,1:T(4,128)S(1)}, s32[8,3]{0,1:T(4,128)}, u32[]{:S(2)}) copy-start(s32[8,3]{0,1:T(4,128)} %param.7) | copy-start | bytes 292
  45.4 35.3 %copy-start.3 = (s32[256]{0:T(256)S(1)}, s32[256]{0:T(256)}, u32[]{:S(2)}) copy-start(s32[256]{0:T(256)} %param.6) | copy-start | bytes 3076
  45.4 108.4 %all-gather.7.cloned.1.call-start = ((), (), s32[]{:S(2)}) async-start(), calls=%async_computation.5 | async-start | bytes 4718592 | tf_op jit(solution)/shard_map/all_gather | solution.py:36
  80.2 104.3 %all-gather.9.cloned.1.call-start = ((), (), s32[]{:S(2)}) async-start(), calls=%async_computation.6 | async-start | bytes 2621440 | tf_op jit(solution)/shard_map/all_gather | solution.py:58
  153.8 7.4 %copy-start.1 = (bf16[256,1024]{1,0:T(8,128)(2,1)S(1)}, bf16[256,1024]{1,0:T(8,128)(2,1)}, u32[]{:S(2)}) copy-start(bf16[256,1024]{1,0:T(8,128)(2,1)} %reduce-scatter.4.cloned.1.call-done) | copy-start | bytes 1572868
  163.5 121.2 %reduce-scatter.6.cloned.1.call-start = ((), (), s32[]{:S(2)}) async-start(), calls=%async_computation.7 | async-start | bytes 4718592 | tf_op jit(solution)/shard_map/reduce_scatter | solution.py:70
  196.3 180.8 %reduce-scatter.8.cloned.1.call-start = ((), (), s32[]{:S(2)}) async-start(), calls=%async_computation.8 | async-start | bytes 4718592 | tf_op jit(solution)/shard_map/reduce_scatter | solution.py:71
Sparse Core Ops, SparseCore 0:
  9.6 25.2 all-gather.4
  45.5 31.4 reduce-scatter.3
  80.3 73.4 all-gather.6
  163.6 20.8 all-gather.8
  196.4 88.2 reduce-scatter.5
  288.8 88.1 reduce-scatter.7
